TPU v7x, 256 devices: a whole 4x4x8 slice. The times are simulated.
256 devices in a mesh: batch: 32 (over z, y), tensor: 8 (over x, core).
Axes of the slice: x: 4, y: 4, z: 8, core: 2. Of those that a mesh axis runs over, the one named last changes fastest.
Arguments:
- tokens: bfloat16 [16384, 8192], P('batch', 'tensor'), may hold values from -6 to 6
- projection_weight: bfloat16 [8192, 4096], P('tensor'), may hold values from -0.0625 to 0.0625
- adapter_input_maps: bfloat16 [128, 8192, 64], P('batch', 'tensor'), may hold values from -0.0625 to 0.0625
- adapter_output_maps: bfloat16 [128, 64, 4096], P('batch', None, 'tensor'), may hold values from -0.75 to 0.75
- adapter_store_row: int32 [128], replicated, may hold values from 0 to 127, as said below
- adapter_lists_by_batch: int32 [32, 32], P('batch'), may hold values from 0 to 127, as said below
- request_list_position: int32 [16384, 1], P('batch'), may hold values from 0 to 31; in each aligned block of 512 rows (0 to 511, 512 to 1023, ...) at most 64 rows name the same one
Outputs:
- output: bfloat16 [16384, 4096], P('batch', 'tensor')
Inputs may be any that keep to these rules, and one draw needn't show every extreme that they name: A permutation: adapter a lives in store row adapter_store_row[a], and store rows o * 4 to (o + 1) * 4 - 1 sit on index o of batch. `adapter_lists_by_batch`: each row lists 32 different adapters; at most 2 of them sit on one index of batch, and in every row some index holds exactly 2. `request_list_position`: among the 512 requests of one batch at most 64 share one list position, and in some batch one position is shared by exactly 64.
All inputs are finite; a program needn't handle non-finite values.
Results may differ from a plain program's by a relative error of at most 0.0047.
Values may be sent and summed in bfloat16 or wider, within the bound.
A program may use at most 128 MiB of HBM per device.

v0:
```python
import jax
import jax.numpy as jnp
from jax import lax
from jax.sharding import PartitionSpec as P

CAP = 2


def list_table(lists, adapter_store_row, owners, loop_depth, capacity):
    rows = adapter_store_row[lists]
    owner = rows // loop_depth
    local = rows % loop_depth
    groups = lists.shape[1]
    same = owner[:, :, None] == owner[:, None, :]
    earlier = jnp.arange(groups)[None, :] < jnp.arange(groups)[:, None]
    ranked = jnp.sum((same & earlier[None]).astype(jnp.int32), axis=2)
    match = (owner[:, :, None, None] == jnp.arange(owners)[None, None, :, None]) & (
        ranked[:, :, None, None] == jnp.arange(capacity)[None, None, None, :]
    )
    table = jnp.sum(jnp.where(match, local[:, :, None, None] + 1, 0), axis=1) - 1
    return (table, owner, ranked)


def body(
    tokens,
    projection_weight,
    adapter_input_maps,
    adapter_output_maps,
    adapter_store_row,
    adapter_lists_by_batch,
    request_list_position,
):
    owners = lax.axis_size("batch")
    loop_depth = adapter_input_maps.shape[0]
    groups = adapter_lists_by_batch.shape[1]
    slots = request_list_position[:, 0]
    table, owner, ranked = list_table(
        adapter_lists_by_batch, adapter_store_row, owners, loop_depth, CAP
    )
    wanted = lax.all_to_all(table[0], "batch", split_axis=0, concat_axis=0, tiled=True)
    adapter_selector = (wanted[:, :, None] == jnp.arange(loop_depth)[None, None, :]).astype(
        jnp.bfloat16
    )
    outgoing_input_maps = jnp.einsum(
        "mwf,fbx->mwbx", adapter_selector, adapter_input_maps, preferred_element_type=jnp.float32
    ).astype(jnp.bfloat16)
    outgoing_output_maps = jnp.einsum(
        "hxd,dms->hxms", adapter_selector, adapter_output_maps, preferred_element_type=jnp.float32
    ).astype(jnp.bfloat16)
    got_a, got_b = (
        lax.all_to_all(outgoing_input_maps, "batch", split_axis=0, concat_axis=0, tiled=True),
        lax.all_to_all(outgoing_output_maps, "batch", split_axis=0, concat_axis=0, tiled=True),
    )
    position = owner[0] * CAP + ranked[0]
    fetched_a = jnp.take(got_a.reshape((-1,) + got_a.shape[2:]), position, axis=0)
    fetched_b = jnp.take(got_b.reshape((-1,) + got_b.shape[2:]), position, axis=0)
    slot_hot = slots[:, None] == jnp.arange(groups)[None, :]
    every_low = jnp.einsum("td,gdr->tgr", tokens, fetched_a, preferred_element_type=jnp.float32)
    partial_low = jnp.sum(jnp.where(slot_hot[:, :, None], every_low, 0.0), axis=1)
    low_rank = lax.psum(partial_low, "tensor").astype(jnp.bfloat16)
    spread = slot_hot[:, :, None].astype(jnp.bfloat16) * low_rank[:, None, :]
    adapted = jnp.einsum("tgr,gro->to", spread, fetched_b, preferred_element_type=jnp.float32)
    base_cols = lax.psum_scatter(
        lax.dot_general(
            projection_weight, tokens, (((0,), (1,)), ((), ())), preferred_element_type=jnp.float32
        ),
        "tensor",
        scatter_dimension=0,
        tiled=True,
    )
    return (base_cols.T + 2.0 * adapted).astype(jnp.bfloat16)


def solution(mesh):
    in_specs = (
        P("batch", "tensor"),
        P("tensor", None),
        P("batch", "tensor", None),
        P("batch", None, "tensor"),
        P(),
        P("batch", None),
        P("batch", None),
    )
    out_specs = P("batch", "tensor")
    return jax.shard_map(body, mesh=mesh, in_specs=in_specs, out_specs=out_specs, check_vma=False)
```

profile of v0, /device:TPU:1, one launch (start us, length us, event | category | flops | bytes accessed | tf_op | source)
XLA Modules:
  0.0 370.5 jit_solution(1277369961605779176)
XLA Ops:
  6.5 0.7 fusion.46
  7.3 1.4 gather_fusion
  8.7 0.2 convert_reduce_fusion
  8.9 0.1 select_reduce_fusion
  9.0 0.1 copy.28
  9.1 20.4 %all_to_all.16 = s32[32,1,2]{2,1,0:T(1,128)S(1)} all-to-all(s32[32,1,2]{2,1,0:T(1,128)S(1)} %copy.28), channel_id=1, replica_groups=mesh['batch'=32,'tensor'=8] {'batch'}, dimensions={0} | all-to-all | bytes 512 | tf_op jit(solution)/shard_map/all_to_all | solution.py:40
  29.5 0.1 copy.29
  29.6 2.3 convolution_convert_fusion.1
  31.9 4.3 %copy.33 = bf16[32,2,64,512]{3,2,1,0:T(8,128)(2,1)} copy(bf16[32,2,64,512]{3,0,2,1:T(8,128)(2,1)S(1)} %convolution_convert_fusion.1) | data formatting | bytes 8388608 | tf_op jit(solution)/shard_map/convert_element_type | solution.py:49
  36.2 5.0 %all-to-all-start.2 = ((bf16[32,2,64,512]{3,2,1,0:T(8,128)(2,1)}), bf16[32,2,64,512]{3,2,1,0:T(8,128)(2,1)}, u32[]{:S(2)}, u32[]{:S(2)}) async-start(bf16[32,2,64,512]{3,2,1,0:T(8,128)(2,1)} %copy.33), calls=%async_computation.3 | async-start | bytes 8388608 | tf_op jit(solution)/shard_map/all_to_all | solution.py:52
  41.2 4.7 %convolution_convert_fusion = bf16[32,2,1024,64]{2,0,3,1:T(8,128)(2,1)} fusion(bf16[4,1024,64]{1,2,0:T(8,128)(2,1)S(1)} %copy-done.1, s32[32,2]{0,1:T(2,128)S(1)} %bitcast.56), kind=kOutput, calls=%fused_computation.3 | convolution fusion | flops 37748992 | bytes 8913152 | tf_op jit(solution)/shard_map/mwf,fbx->mwbx/dot_general | solution.py:44
  46.0 11.3 %copy.31 = bf16[32,2,1024,64]{2,3,1,0:T(8,128)(2,1)} copy(bf16[32,2,1024,64]{2,0,3,1:T(8,128)(2,1)} %convolution_convert_fusion) | data formatting | bytes 16777216 | tf_op jit(solution)/shard_map/convert_element_type | solution.py:46
  57.3 76.7 %all-to-all-done.2 = bf16[32,2,64,512]{3,2,1,0:T(8,128)(2,1)} async-done(((bf16[32,2,64,512]{3,2,1,0:T(8,128)(2,1)}), bf16[32,2,64,512]{3,2,1,0:T(8,128)(2,1)}, u32[]{:S(2)}, u32[]{:S(2)}) %all-to-all-start.2) | async-done | bytes 4194336 | tf_op jit(solution)/shard_map/all_to_all | solution.py:52
  134.0 6.8 %all-to-all-start.1 = ((bf16[32,2,1024,64]{2,3,1,0:T(8,128)(2,1)}), bf16[32,2,1024,64]{2,3,1,0:T(8,128)(2,1)}, u32[]{:S(2)}, u32[]{:S(2)}) async-start(bf16[32,2,1024,64]{2,3,1,0:T(8,128)(2,1)} %copy.31), calls=%async_computation.2 | async-start | bytes 16777216 | tf_op jit(solution)/shard_map/all_to_all | solution.py:51
  140.8 0.2 reduce-scatter.2.cloned.1.call-start
  141.0 10.4 %fusion.51 = f32[4096,512]{1,0:T(8,128)} fusion(bf16[1024,4096]{1,0:T(8,128)(2,1)} %param.8, bf16[512,1024]{1,0:T(8,128)(2,1)S(1)} %copy-done), kind=kOutput, calls=%fused_computation.62 | convolution fusion | flops 4294967296 | bytes 17825792 | tf_op jit(solution)/shard_map/dot_general | solution.py:64
  151.5 0.6 copy-done.2
  152.1 2.9 gather_fusion.2
  155.0 166.5 %all-to-all-done.1 = bf16[32,2,1024,64]{2,3,1,0:T(8,128)(2,1)} async-done(((bf16[32,2,1024,64]{2,3,1,0:T(8,128)(2,1)}), bf16[32,2,1024,64]{2,3,1,0:T(8,128)(2,1)}, u32[]{:S(2)}, u32[]{:S(2)}) %all-to-all-start.1) | async-done | bytes 8388640 | tf_op jit(solution)/shard_map/all_to_all | solution.py:51
  321.5 6.2 %gather_fusion.1 = bf16[32,1024,64]{1,2,0:T(8,128)(2,1)} fusion(bf16[64,1024,64]{1,2,0:T(8,128)(2,1)} %bitcast.8, s32[1024]{0:T(1024)S(1)} %pad_clamp_fusion), kind=kCustom, calls=%fused_computation.1 | custom fusion | bytes 8388736 | tf_op jit(solution)/shard_map/jit(_take)/gather | solution.py:55
  327.7 4.7 %fusion = f32[512,64]{0,1:T(8,128)S(1)} fusion(pred[512,32]{0,1:T(8,128)(4,1)S(1)} %get-tuple-element.6, bf16[32,1024,64]{1,2,0:T(8,128)(2,1)} %gather_fusion.1, pred[32]{0:T(512)(128)(4,1)S(1)} %compare_and_fusion, bf16[512,1024]{1,0:T(8,128)(2,1)S(1)} %copy-done), kind=kOutput, calls=%fused_computation.5 | convolution fusion | flops 2151645184 | bytes 5390368 | tf_op jit(solution)/shard_map/td,gdr->tgr/dot_general | solution.py:58
  332.4 25.6 %all-reduce.1 = bf16[512,64]{0,1:T(8,128)(2,1)S(1)} all-reduce(f32[512,64]{0,1:T(8,128)S(1)} %fusion), channel_id=1, replica_groups=mesh['batch'=32,'tensor'=8] {'tensor'}, use_global_device_ids=true, to_apply=%region_4.5 | all-reduce | flops 32768 | bytes 196608 | tf_op jit(solution)/shard_map/psum | solution.py:60
  358.0 3.7 fusion.24
  361.6 2.0 copy.35
  (16 shorter events, 0.2 us)
Async XLA Ops:
  6.5 134.5 %copy-start = (bf16[512,1024]{1,0:T(8,128)(2,1)S(1)}, bf16[512,1024]{1,0:T(8,128)(2,1)}, u32[]{:S(2)}) copy-start(bf16[512,1024]{1,0:T(8,128)(2,1)} %param.7) | copy-start | bytes 3145732
  36.2 5.0 %copy-start.1 = (bf16[4,1024,64]{1,2,0:T(8,128)(2,1)S(1)}, bf16[4,1024,64]{1,2,0:T(8,128)(2,1)}, u32[]{:S(2)}) copy-start(bf16[4,1024,64]{1,2,0:T(8,128)(2,1)} %param.9) | copy-start | bytes 1572868
  36.2 97.7 %all-to-all-start.2 = ((bf16[32,2,64,512]{3,2,1,0:T(8,128)(2,1)}), bf16[32,2,64,512]{3,2,1,0:T(8,128)(2,1)}, u32[]{:S(2)}, u32[]{:S(2)}) async-start(bf16[32,2,64,512]{3,2,1,0:T(8,128)(2,1)} %copy.33), calls=%async_computation.3 | async-start | bytes 8388608 | tf_op jit(solution)/shard_map/all_to_all | solution.py:52
  134.0 187.5 %all-to-all-start.1 = ((bf16[32,2,1024,64]{2,3,1,0:T(8,128)(2,1)}), bf16[32,2,1024,64]{2,3,1,0:T(8,128)(2,1)}, u32[]{:S(2)}, u32[]{:S(2)}) async-start(bf16[32,2,1024,64]{2,3,1,0:T(8,128)(2,1)} %copy.31), calls=%async_computation.2 | async-start | bytes 16777216 | tf_op jit(solution)/shard_map/all_to_all | solution.py:51
  140.8 217.2 %reduce-scatter.2.cloned.1.call-start = ((), (), s32[]{:S(2)}) async-start(), calls=%async_computation.4 | async-start | bytes 9437184 | tf_op jit(solution)/shard_map/reduce_scatter | solution.py:63
  151.4 0.7 copy-start.2
Sparse Core Ops, SparseCore 0:
  151.5 57.8 reduce-scatter.1
where the time goes:
time: 375 us; the launch traced here: 371 us
  waiting for transfers between devices  243 us (65%)
  blocking collectives  46 us (12%)
  local copies, waits for them, and re-layouts  28.8 us (8%)
  matrix products  25.8 us (7%)
  between operations  13.5 us (4%)
  starting transfers between devices  12 us (3%)
    all_to_all x1, waiting for transfers between devices, body(): lax.all_to_all(outgoing_input_maps, 'batch', split_axis=0, concat_axis=0,...  167 us
    all_to_all x1, waiting for transfers between devices, body(): lax.all_to_all(outgoing_output_maps, 'batch', split_axis=0, concat_axis=0...  76.7 us
    psum x1, blocking collectives, body(): low_rank = lax.psum(partial_low, 'tensor').astype(jnp.bfloat16)  25.6 us
    all_to_all x1, blocking collectives, body(): lax.all_to_all(table[0], 'batch', split_axis=0, concat_axis=0, tiled=True)  20.4 us
    convert_element_type x1, local copies, waits for them, and re-layouts, body(): outgoing_input_maps = jnp.einsum('mwf,fbx->mwbx', adapter_selector, adapt...  11.3 us
    dot_general x1, matrix products, body(): lax.dot_general(projection_weight, tokens, (((0,), (1,)), ((), ())), pref...  10.4 us
  transfers between devices with their start and end apart: 3, of which 2 were waited for; matrix products, arithmetic and copies ran while one was open for 11% of the time, Pallas kernels for 0%

commit v1 on v0

v1 whole, which is shorter than its diff:
```python
import jax
import jax.numpy as jnp
from jax import lax
from jax.experimental import pallas as pl
from jax.experimental.pallas import tpu as pltpu
from jax.sharding import PartitionSpec as P

MESH = pl.DeviceIdType.MESH
BF = jnp.bfloat16
F32 = jnp.float32
NT = (((1,), (1,)), ((), ()))
PLUS, MINUS = 0, 1
STREAM_A, STREAM_B0, STREAM_B1 = 0, 1, 2


def kernel(
    tok_h, w_h, a_h, b_h, store_ref, list_ref, pos_ref, out_ref,
    tok_all, a_all, b_all, s_all, s_bc, wbuf, acc,
    mate_send, mate_recv, q, base_own, x_half, x_recv,
    packed, part_recv, low_all, spread, y_send, y_half, y_recv, own_adapted,
    local_sem, w_sem, z_send, z_recv, yt_send, yt_recv, s_send, s_recv,
    m_send, m_recv, x_send_sem, x_recv_sem, p_send, p_recv, g_send, g_recv,
    r_send, r_recv,
):
    b = lax.axis_index("batch")
    t = lax.axis_index("tensor")
    z, y = lax.div(b, 4), lax.rem(b, 4)
    x, c = lax.div(t, 2), lax.rem(t, 2)

    def at_z(d):
        return lax.rem(z + d + 8, 8)

    z_dev = ((at_z(1) * 4 + y, t), (at_z(-1) * 4 + y, t))
    y_dev = ((z * 4 + lax.rem(y + 1, 4), t), (z * 4 + lax.rem(y + 3, 4), t))
    y_far = (z * 4 + lax.rem(y + 2, 4), t)
    x_dev = ((b, lax.rem(x + 1, 4) * 2 + c), (b, lax.rem(x + 3, 4) * 2 + c))
    mate = (b, x * 2 + 1 - c)
    others = [(b, lax.rem(t + k, 8)) for k in range(1, 8)]

    started = []

    def go(copy):
        copy.start()
        started.append(copy)

    def remote(src, dst, send, recv, device):
        return pltpu.make_async_remote_copy(
            src_ref=src, dst_ref=dst, send_sem=send, recv_sem=recv,
            device_id=device, device_id_type=MESH,
        )

    tok_local = [
        pltpu.make_async_copy(tok_h.at[pl.ds(256 * i, 256)], tok_all.at[i], local_sem.at[i])
        for i in range(2)
    ]
    a_local = pltpu.make_async_copy(a_h, a_all.at[0], local_sem.at[2])
    b_local = [
        pltpu.make_async_copy(
            b_h.at[:, pl.ds(256 * n, 256)], b_all.at[n, pl.ds(0, 256)], local_sem.at[3 + n]
        )
        for n in range(2)
    ]
    chips = [lax.rem(x + d, 4) for d in (2, 1, 3, 0)]
    w_local = []
    for j in range(8):
        column = (chips[j % 4] * 2 + (1 - c if j < 4 else c)) * 512
        w_local.append(
            pltpu.make_async_copy(
                w_h.at[:, pl.ds(pl.multiple_of(column, 512), 512)], wbuf.at[j], w_sem.at[j]
            )
        )
    for copy in tok_local + w_local[:2] + [a_local] + w_local[2:] + b_local:
        copy.start()

    barrier = pltpu.get_barrier_semaphore()
    partners = [z_dev[0], z_dev[1], y_dev[0], y_dev[1], y_far] + others
    for device in partners:
        pl.semaphore_signal(barrier, inc=1, device_id=device, device_id_type=MESH)

    list_row = jnp.broadcast_to(list_ref[...].astype(F32), (32, 32))
    eye = lax.broadcasted_iota(jnp.int32, (32, 32), 0) == lax.broadcasted_iota(jnp.int32, (32, 32), 1)
    list_col = jnp.sum(jnp.where(eye, list_row, 0.0), axis=1, keepdims=True)
    lane_a = lax.broadcasted_iota(jnp.int32, (32, 128), 1).astype(F32)
    rows_col = jnp.sum(
        jnp.where(lane_a == list_col, jnp.broadcast_to(store_ref[...].astype(F32), (32, 128)), 0.0),
        axis=1, keepdims=True,
    )
    hot = lax.broadcasted_iota(jnp.int32, (32, 512), 0) == jnp.broadcast_to(pos_ref[...], (32, 512))
    s_row = jnp.sum(jnp.where(hot, jnp.broadcast_to(rows_col, (32, 512)), 0.0), axis=0, keepdims=True)
    s_all[0] = jnp.broadcast_to(s_row, (8, 512))

    pl.semaphore_wait(barrier, len(partners))

    s_copies = [
        remote(s_all.at[0], s_all.at[slot], s_send.at[slot - 1], s_recv.at[slot - 1], device)
        for slot, device in ((1, y_dev[0]), (2, y_dev[1]), (3, y_far))
    ]

    def z_place(stream, slot, half):
        if stream == STREAM_A:
            return a_all.at[slot, pl.ds(half * 128, 128)]
        return b_all.at[stream - 1, pl.ds(slot * 256 + half * 128, 128)]

    def z_own(stream, half):
        if stream == STREAM_A:
            return a_h.at[pl.ds(half * 128, 128)]
        return b_h.at[pl.ds(half * 128, 128), pl.ds(256 * (stream - 1), 256)]

    def z_slot(way, d):
        return 7 if d == 4 else d + 3 * way

    def z_copy(stream, way, k):
        d, half = k // 2 + 1, (k % 2) ^ way
        src = z_own(stream, half) if d == 1 else z_place(stream, z_slot(way, d - 1), half)
        i = stream * 14 + way * 7 + k
        return remote(src, z_place(stream, z_slot(way, d), half), z_send.at[i], z_recv.at[i], z_dev[way])

    z_all = [[[z_copy(s, w, k) for k in range(7)] for w in range(2)] for s in range(3)]

    def z_begin(stream):
        for k in range(2):
            for way in range(2):
                go(z_all[stream][way][k])

    def z_serve(stream, k):
        for way in range(2):
            z_all[stream][way][k].wait_recv()
            if k < 5:
                go(z_all[stream][way][k + 2])

    def y_copy(way, k):
        half = (k % 2) ^ way
        if k < 2:
            src, dst = tok_h.at[pl.ds(256 * half, 256)], tok_all.at[2 * (1 + way) + half]
        else:
            src, dst = tok_all.at[2 * (1 + way) + half], tok_all.at[6 + half]
        return remote(src, dst, yt_send.at[way * 3 + k], yt_recv.at[way * 3 + k], y_dev[way])

    y_tok = [[y_copy(w, k) for k in range(3)] for w in range(2)]

    for copy in s_copies:
        go(copy)
    z_begin(STREAM_A)
    for k in range(2):
        for way in range(2):
            go(y_tok[way][k])

    for copy in tok_local:
        copy.wait()

    mate_copies = [
        remote(mate_send.at[j], mate_recv.at[j], m_send.at[j], m_recv.at[j], mate) for j in range(4)
    ]

    def base_tile(i, j):
        return jnp.dot(tok_all[i], wbuf[j], preferred_element_type=F32)

    for j in range(4):
        w_local[j].wait()

        @pl.loop(0, 2)
        def _(i):
            mate_send[j, i] = base_tile(i, j).astype(BF)

        go(mate_copies[j])

    def base_mine(j):
        w_local[4 + j].wait()
        mate_copies[j].wait_recv()

        @pl.loop(0, 2)
        def _(i):
            total = base_tile(i, 4 + j) + mate_recv[j, i].astype(F32)
            if j < 3:
                q[j, i] = total.astype(BF)
            else:
                base_own[i] = total

    def x_copy(n, src, dst, way):
        return remote(src, dst, x_send_sem.at[n], x_recv_sem.at[n], x_dev[way])

    x_first = [x_copy(w, q.at[0, w], x_half.at[w], w) for w in range(2)]
    x_plain = [x_copy(2 + w, q.at[1 + w, 1 - w], x_recv.at[w, 1 - w], w) for w in range(2)]
    x_added = [x_copy(4 + w, q.at[1 + w, w], x_recv.at[w, w], w) for w in range(2)]

    base_mine(0)
    for copy in x_first:
        go(copy)
    base_mine(1)
    go(x_plain[0])
    base_mine(2)
    go(x_plain[1])
    z_serve(STREAM_A, 0)
    base_mine(3)

    for copy in s_copies:
        copy.wait_recv()
    for slot in range(4):
        for block in range(4):
            row = s_all[slot, 0:1, 128 * block:128 * (block + 1)]
            tile = jnp.broadcast_to(row, (128, 128)).T
            s_bc[2 * slot + block // 2, 128 * (block % 2):128 * (block % 2 + 1)] = tile

    z_serve(STREAM_A, 1)
    for way in range(2):
        y_tok[way][0].wait_recv()
        go(y_tok[way][2])
    for way in range(2):
        x_first[way].wait_recv()
        q[1 + way, way] = (q[1 + way, way].astype(F32) + x_half[way].astype(F32)).astype(BF)
        go(x_added[way])

    quarter = lax.broadcasted_iota(jnp.int32, (256, 128), 1) // 64

    def first_row(slot):
        d = 4 if slot == 7 else (-slot if slot < 4 else slot - 3)
        return at_z(d) * 16 + y * 4

    def low(slot, lowest, highest):
        rows = [(first_row(slot) + 2 * h + quarter).astype(F32) for h in range(2)]

        @pl.loop(lowest, highest)
        def _(i):
            product = lax.dot_general(tok_all[i], a_all[slot], NT, preferred_element_type=F32)
            for h in range(2):
                kept = jnp.where(s_bc[i] == rows[h], product[:, 128 * h:128 * (h + 1)], 0.0)
                if slot == 0:
                    acc[i, :, 128 * h:128 * (h + 1)] = kept
                else:
                    acc[i, :, 128 * h:128 * (h + 1)] += kept

    a_local.wait()
    for slot in (0, 1, 4):
        low(slot, 0, 2)
    z_serve(STREAM_A, 2)
    z_serve(STREAM_A, 3)
    for way in range(2):
        y_tok[way][1].wait_recv()
    for slot in (0, 1, 4):
        low(slot, 2, 6)
    for slot in (2, 5):
        low(slot, 0, 6)
    z_serve(STREAM_A, 4)
    z_serve(STREAM_A, 5)
    z_begin(STREAM_B0)
    for way in range(2):
        y_tok[way][2].wait_recv()
    for slot in (0, 1, 4, 2, 5):
        low(slot, 6, 8)
    for slot in (3, 6):
        low(slot, 0, 8)
    z_serve(STREAM_A, 6)
    z_begin(STREAM_B1)
    low(7, 0, 8)

    lane = lax.broadcasted_iota(jnp.int32, (256, 128), 1)

    def folded(i):
        h = acc[i, :, 0:128] + acc[i, :, 128:256]
        return h + pltpu.roll(h, 64, 1)

    @pl.loop(0, 4)
    def _(i):
        both = jnp.where(lane < 64, folded(i), folded(i + 4))
        packed[2 * i] = both[0:128]
        packed[2 * i + 1] = both[128:256]

    p_copies = [
        remote(packed.at[lax.rem(t + k, 8)], part_recv.at[k - 1], p_send.at[k - 1], p_recv.at[k - 1], others[k - 1])
        for k in range(1, 8)
    ]
    for copy in p_copies:
        go(copy)
    for k in range(3):
        z_serve(STREAM_B0, k)
    for copy in p_copies:
        copy.wait_recv()
    total = packed[t]
    for k in range(7):
        total += part_recv[k]
    low_all[t] = total.astype(BF)
    g_copies = [
        remote(low_all.at[t], low_all.at[t], g_send.at[k - 1], g_recv.at[k - 1], others[k - 1])
        for k in range(1, 8)
    ]
    for copy in g_copies:
        go(copy)
    for k in range(3, 5):
        z_serve(STREAM_B0, k)
    z_serve(STREAM_B1, 0)
    z_serve(STREAM_B1, 1)
    for k in range(1, 8):
        remote(
            low_all.at[t], low_all.at[lax.rem(t + 8 - k, 8)], g_send.at[k - 1], g_recv.at[k - 1], others[k - 1]
        ).wait_recv()

    @pl.loop(0, 8)
    def _(i):
        r = lax.rem(i, 4)
        v = jnp.concatenate([low_all[2 * r], low_all[2 * r + 1]], axis=0).astype(F32)
        turned = pltpu.roll(v, 64, 1)
        both = jnp.where((lane < 64) == (i < 4), v, turned)
        rows = s_bc[i]
        for slot in range(8):
            for h in range(2):
                want = (first_row(slot) + 2 * h + quarter).astype(F32)
                column = slot * 256 + 128 * h
                spread[i, :, column:column + 128] = jnp.where(rows == want, both, 0.0).astype(BF)

    for copy in b_local:
        copy.wait()

    def r_copy(n, half, index, src, dst, way):
        i = n * 6 + index
        return remote(src, dst, r_send.at[i], r_recv.at[i], y_dev[way])

    r_first = [[r_copy(n, w, w, y_send.at[n, 4 + w], y_half.at[n, w], w) for w in range(2)] for n in range(2)]
    r_plain = [
        [r_copy(n, 1 - w, 2 + w, y_send.at[n, 2 * (1 - w) + 1 - w], y_recv.at[n, w, 1 - w], w) for w in range(2)]
        for n in range(2)
    ]
    r_added = [
        [r_copy(n, w, 4 + w, y_send.at[n, 2 * (1 - w) + w], y_recv.at[n, w, w], w) for w in range(2)]
        for n in range(2)
    ]

    def adapted(n, i):
        return jnp.dot(spread[i], b_all[n], preferred_element_type=F32)

    def send_back(n):
        @pl.loop(6, 8)
        def _(i):
            y_send[n, i - 2] = adapted(n, i).astype(BF)

        for way in range(2):
            go(r_first[n][way])

        @pl.loop(2, 6)
        def _(i):
            y_send[n, i - 2] = adapted(n, i).astype(BF)

        for way in range(2):
            go(r_plain[n][way])

    def send_added(n):
        for way in range(2):
            r_first[n][way].wait_recv()
            place = 2 * (1 - way) + way
            y_send[n, place] = (y_send[n, place].astype(F32) + y_half[n, way].astype(F32)).astype(BF)
            go(r_added[n][way])

    def mine(n):
        @pl.loop(0, 2)
        def _(i):
            own_adapted[n, i] = adapted(n, i)

    def finish(n):
        for way in range(2):
            r_plain[n][way].wait_recv()
            r_added[n][way].wait_recv()
        for i in range(2):
            columns = pl.ds(256 * n, 256)
            base = base_own[i, :, columns] + (
                x_recv[0, i, :, columns].astype(F32) + x_recv[1, i, :, columns].astype(F32)
            )
            extra = own_adapted[n, i] + (y_recv[n, 0, i].astype(F32) + y_recv[n, 1, i].astype(F32))
            out_ref[pl.ds(256 * i, 256), columns] = (base + 2.0 * extra).astype(BF)

    z_serve(STREAM_B0, 5)
    z_serve(STREAM_B0, 6)
    z_serve(STREAM_B1, 2)
    send_back(0)
    z_serve(STREAM_B1, 3)
    z_serve(STREAM_B1, 4)
    send_added(0)
    mine(0)
    z_serve(STREAM_B1, 5)
    z_serve(STREAM_B1, 6)
    send_back(1)
    mine(1)
    send_added(1)
    for way in range(2):
        x_plain[way].wait_recv()
        x_added[way].wait_recv()
    finish(0)
    finish(1)
    for copy in started:
        copy.wait_send()


def body(
    tokens,
    projection_weight,
    adapter_input_maps,
    adapter_output_maps,
    adapter_store_row,
    adapter_lists_by_batch,
    request_list_position,
):
    dma = pltpu.SemaphoreType.DMA
    vmem = pltpu.VMEM
    hbm = pl.BlockSpec(memory_space=pl.ANY)
    near = pl.BlockSpec(memory_space=pltpu.VMEM)
    return pl.pallas_call(
        kernel,
        out_shape=jax.ShapeDtypeStruct((512, 512), BF),
        in_specs=[hbm] * 4 + [near] * 3,
        out_specs=near,
        scratch_shapes=[
            vmem((8, 256, 1024), BF),
            vmem((8, 256, 1024), BF),
            vmem((2, 2048, 256), BF),
            vmem((4, 8, 512), F32),
            vmem((8, 256, 128), F32),
            vmem((8, 1024, 512), BF),
            vmem((8, 256, 256), F32),
            vmem((4, 2, 256, 512), BF),
            vmem((4, 2, 256, 512), BF),
            vmem((3, 2, 256, 512), BF),
            vmem((2, 256, 512), F32),
            vmem((2, 256, 512), BF),
            vmem((2, 2, 256, 512), BF),
            vmem((8, 128, 128), F32),
            vmem((7, 128, 128), F32),
            vmem((8, 128, 128), BF),
            vmem((8, 256, 2048), BF),
            vmem((2, 6, 256, 256), BF),
            vmem((2, 2, 256, 256), BF),
            vmem((2, 2, 2, 256, 256), BF),
            vmem((2, 2, 256, 256), F32),
            dma((5,)), dma((8,)), dma((42,)), dma((42,)), dma((6,)), dma((6,)), dma((3,)), dma((3,)),
            dma((4,)), dma((4,)), dma((6,)), dma((6,)), dma((7,)), dma((7,)), dma((7,)), dma((7,)),
            dma((12,)), dma((12,)),
        ],
        compiler_params=pltpu.CompilerParams(
            collective_id=0, has_side_effects=True, vmem_limit_bytes=56 * 1024 * 1024
        ),
        cost_estimate=pl.CostEstimate(flops=17_200_000_000, bytes_accessed=13_000_000, transcendentals=0),
    )(
        tokens,
        projection_weight,
        jnp.swapaxes(adapter_input_maps, 1, 2).reshape(256, 1024),
        adapter_output_maps.reshape(256, 512),
        adapter_store_row.reshape(1, 128),
        adapter_lists_by_batch,
        request_list_position.reshape(1, 512),
    )


def solution(mesh):
    in_specs = (
        P("batch", "tensor"),
        P("tensor", None),
        P("batch", "tensor", None),
        P("batch", None, "tensor"),
        P(),
        P("batch", None),
        P("batch", None),
    )
    out_specs = P("batch", "tensor")
    return jax.shard_map(body, mesh=mesh, in_specs=in_specs, out_specs=out_specs, check_vma=False)
```

time: 375 us -> 99.1 us (0.26); the launches traced: 371 us -> 98.9 us
  waiting for transfers between devices: 243 us -> 0 us
  Pallas kernels: 0 us -> 97.1 us
  blocking collectives: 46 us -> 0 us
  local copies, waits for them, and re-layouts: 28.8 us -> 1.87 us
  matrix products: 25.8 us -> 0 us
  between operations: 13.5 us -> 0.01 us
  starting transfers between devices: 12 us -> 0 us
    all_to_all x2 -> x0, waiting for transfers between devices: 243 us -> none  [the longest x1 167 us: body(): lax.all_to_all(outgoing_input_maps, 'batch', split_axis=0, concat_axis=0,...]
    pallas_call x0 -> x1, Pallas kernels: none -> 97.1 us  [body(): pl.pallas_call(kernel, out_shape=jax.ShapeDtypeStruct((512, 512), BF), in...]
    dot_general x5 -> x0, matrix products: 25.8 us -> none  [the longest x1 10.4 us: body(): lax.dot_general(projection_weight, tokens, (((0,), (1,)), ((), ())), pref...]
    psum x1 -> x0, blocking collectives: 25.6 us -> none  [body(): low_rank = lax.psum(partial_low, 'tensor').astype(jnp.bfloat16)]
    all_to_all x1 -> x0, blocking collectives: 20.4 us -> none  [body(): lax.all_to_all(table[0], 'batch', split_axis=0, concat_axis=0, tiled=True)]
    convert_element_type x3 -> x0, local copies, waits for them, and re-layouts: 17.7 us -> none  [the longest x1 11.3 us: body(): outgoing_input_maps = jnp.einsum('mwf,fbx->mwbx', adapter_selector, adapt...]
    all_to_all x2 -> x0, starting transfers between devices: 11.8 us -> none  [the longest x1 6.8 us: body(): lax.all_to_all(outgoing_input_maps, 'batch', split_axis=0, concat_axis=0,...]
    gather x3 -> x0, local copies, waits for them, and re-layouts: 10.4 us -> none  [the longest x1 6.17 us: body(): jnp.take(got_a.reshape((-1,) + got_a.shape[2:]), position, axis=0)]
  transfers between devices with their start and end apart: 3 -> 0, of which waited for: 2 -> 0; matrix products, arithmetic and copies ran while one was open for 11% -> 0% of each run, Pallas kernels for 0% -> 0%
where the time goes in v1:
time: 99.1 us; the launch traced here: 98.9 us
  Pallas kernels  97.1 us (98%)
  local copies, waits for them, and re-layouts  1.87 us (2%)
    pallas_call x1, Pallas kernels, body(): pl.pallas_call(kernel, out_shape=jax.ShapeDtypeStruct((512, 512), BF), in...  97.1 us

profile of v1, /device:TPU:1, one launch (start us, length us, event | category | flops | bytes accessed | tf_op | source)
XLA Modules:
  0.0 98.9 jit_solution(1659347308073190745)
XLA Ops:
  0.0 97.1 %shard_map.73 = bf16[512,512]{1,0:T(8,128)(2,1)} custom-call(bf16[512,1024]{1,0:T(8,128)(2,1)} %tok_h.1, bf16[1024,4096]{1,0:T(8,128)(2,1)} %w_h.1, bf16[256,1024]{1,0:T(8,128)(2,1)} %bitcast.6, bf16[256,512]{1,0:T(8,128)(2,1)} %bitcast.7, s32[1,128]{1,0:T(1,128)} %bitcast.9, s32[1,32]{1,0:T(1,128)} %list_ref.1, s32[1,512]{1,0:T(1,128)} %bitcast.8), custom_call_target="tpu_custom_call" | custom-call | flops 17200001024 | bytes 13000000 | tf_op jit(solution)/shard_map/pallas_call | solution.py:404
  97.1 1.9 %copy.9 = bf16[512,512]{1,0:T(8,128)(2,1)} copy(bf16[512,512]{1,0:T(8,128)(2,1)} %shard_map.73) | data formatting | bytes 1048576

commit v2 on v1

v2 whole, which is shorter than its diff:
```python
import jax
import jax.numpy as jnp
from jax import lax
from jax.experimental import pallas as pl
from jax.experimental.pallas import tpu as pltpu
from jax.sharding import PartitionSpec as P

MESH = pl.DeviceIdType.MESH
BF = jnp.bfloat16
F32 = jnp.float32
NT = (((1,), (1,)), ((), ()))
PLUS, MINUS = 0, 1
STREAM_A = 0
CUTS = ((0, 256), (256, 256))


def kernel(
    tok_h, w_h, a_h, b_h, store_ref, list_ref, pos_ref, out_ref,
    tok_all, a_all, b_all_0, b_all_1, s_all, s_bc, wbuf, acc,
    mate_send, mate_recv, q, base_own, x_half, x_recv,
    packed_0, packed_1, part_0, part_1, low_0, low_1, spread,
    y_send_0, y_half_0, y_recv_0, own_0, y_send_1, y_half_1, y_recv_1, own_1,
    local_sem, w_sem, z_send, z_recv, yt_send, yt_recv, s_send, s_recv,
    m_send, m_recv, x_send_sem, x_recv_sem, p_send, p_recv, g_send, g_recv,
    r_send, r_recv,
):
    b_all = (b_all_0, b_all_1)
    packed, part_recv, low_all = (packed_0, packed_1), (part_0, part_1), (low_0, low_1)
    y_send, y_half = (y_send_0, y_send_1), (y_half_0, y_half_1)
    y_recv, own_adapted = (y_recv_0, y_recv_1), (own_0, own_1)
    b = lax.axis_index("batch")
    t = lax.axis_index("tensor")
    z, y = lax.div(b, 4), lax.rem(b, 4)
    x, c = lax.div(t, 2), lax.rem(t, 2)

    def at_z(d):
        return lax.rem(z + d + 8, 8)

    z_dev = ((at_z(1) * 4 + y, t), (at_z(-1) * 4 + y, t))
    y_dev = ((z * 4 + lax.rem(y + 1, 4), t), (z * 4 + lax.rem(y + 3, 4), t))
    y_far = (z * 4 + lax.rem(y + 2, 4), t)
    x_dev = ((b, lax.rem(x + 1, 4) * 2 + c), (b, lax.rem(x + 3, 4) * 2 + c))
    mate = (b, x * 2 + 1 - c)
    others = [(b, lax.rem(t + k, 8)) for k in range(1, 8)]

    started = []

    def go(copy):
        copy.start()
        started.append(copy)

    def remote(src, dst, send, recv, device):
        return pltpu.make_async_remote_copy(
            src_ref=src, dst_ref=dst, send_sem=send, recv_sem=recv,
            device_id=device, device_id_type=MESH,
        )

    tok_local = [pltpu.make_async_copy(tok_h, tok_all.at[0], local_sem.at[0])]
    a_local = pltpu.make_async_copy(a_h, a_all.at[0], local_sem.at[2])
    b_local = [
        pltpu.make_async_copy(
            b_h.at[:, pl.ds(*CUTS[n])], b_all[n].at[pl.ds(0, 256)], local_sem.at[3 + n]
        )
        for n in range(2)
    ]
    chips = [lax.rem(x + d, 4) for d in (2, 1, 3, 0)]
    w_local = []
    for j in range(8):
        column = (chips[j % 4] * 2 + (1 - c if j < 4 else c)) * 512
        w_local.append(
            pltpu.make_async_copy(
                w_h.at[:, pl.ds(pl.multiple_of(column, 512), 512)], wbuf.at[j], w_sem.at[j]
            )
        )
    for copy in tok_local + w_local[:2] + [a_local] + w_local[2:] + b_local:
        copy.start()

    barrier = pltpu.get_barrier_semaphore()
    partners = [z_dev[0], z_dev[1], y_dev[0], y_dev[1], y_far] + others
    for device in partners:
        pl.semaphore_signal(barrier, inc=1, device_id=device, device_id_type=MESH)

    list_row = jnp.broadcast_to(list_ref[...].astype(F32), (32, 32))
    eye = lax.broadcasted_iota(jnp.int32, (32, 32), 0) == lax.broadcasted_iota(jnp.int32, (32, 32), 1)
    list_col = jnp.sum(jnp.where(eye, list_row, 0.0), axis=1, keepdims=True)
    lane_a = lax.broadcasted_iota(jnp.int32, (32, 128), 1).astype(F32)
    rows_col = jnp.sum(
        jnp.where(lane_a == list_col, jnp.broadcast_to(store_ref[...].astype(F32), (32, 128)), 0.0),
        axis=1, keepdims=True,
    )
    hot = lax.broadcasted_iota(jnp.int32, (32, 512), 0) == jnp.broadcast_to(pos_ref[...], (32, 512))
    s_row = jnp.sum(jnp.where(hot, jnp.broadcast_to(rows_col, (32, 512)), 0.0), axis=0, keepdims=True)
    s_all[0] = jnp.broadcast_to(s_row, (8, 512))

    pl.semaphore_wait(barrier, len(partners))

    s_copies = [
        remote(s_all.at[0], s_all.at[slot], s_send.at[slot - 1], s_recv.at[slot - 1], device)
        for slot, device in ((1, y_dev[0]), (2, y_dev[1]), (3, y_far))
    ]

    def z_rows(way, k):
        return k // 2 + 1, ((k % 2) ^ way) * 128, 128

    def z_place(stream, slot, row, rows):
        if stream == STREAM_A:
            return a_all.at[slot, pl.ds(row, rows)]
        return b_all[stream - 1].at[pl.ds(slot * 256 + row, rows)]

    def z_own(stream, row, rows):
        if stream == STREAM_A:
            return a_h.at[pl.ds(row, rows)]
        return b_h.at[pl.ds(row, rows), pl.ds(*CUTS[stream - 1])]

    def z_slot(way, d):
        return 7 if d == 4 else d + 3 * way

    def z_copy(stream, way, k):
        d, row, rows = z_rows(way, k)
        src = z_own(stream, row, rows) if d == 1 else z_place(stream, z_slot(way, d - 1), row, rows)
        i = stream * 14 + way * 7 + k
        return remote(
            src, z_place(stream, z_slot(way, d), row, rows), z_send.at[i], z_recv.at[i], z_dev[way]
        )

    z_all = [[[z_copy(s, w, k) for k in range(7)] for w in range(2)] for s in range(3)]

    def z_begin(stream, *steps):
        for k in steps:
            for way in range(2):
                go(z_all[stream][way][k])

    def z_serve(stream, k):
        for way in range(2):
            z_all[stream][way][k].wait_recv()
            if k < 5:
                go(z_all[stream][way][k + 2])

    def y_copy(way, k):
        rows = pl.ds(256 * ((k % 2) ^ way), 256)
        if k < 2:
            src, dst = tok_h.at[rows], tok_all.at[1 + way, rows]
        else:
            src, dst = tok_all.at[1 + way, rows], tok_all.at[3, rows]
        return remote(src, dst, yt_send.at[way * 3 + k], yt_recv.at[way * 3 + k], y_dev[way])

    y_tok = [[y_copy(w, k) for k in range(3)] for w in range(2)]

    for copy in s_copies:
        go(copy)
    z_begin(STREAM_A, 0, 1)
    for k in range(2):
        for way in range(2):
            go(y_tok[way][k])

    for copy in tok_local:
        copy.wait()

    mate_copies = [
        remote(mate_send.at[j], mate_recv.at[j], m_send.at[j], m_recv.at[j], mate) for j in range(4)
    ]

    def base_part(j):
        return jnp.dot(tok_all[0], wbuf[j], preferred_element_type=F32)

    for j in range(4):
        w_local[j].wait()

        part = base_part(j).astype(BF)
        mate_send[j, 0] = part[0:256]
        mate_send[j, 1] = part[256:512]

        go(mate_copies[j])

    def base_mine(j):
        w_local[4 + j].wait()
        mate_copies[j].wait_recv()

        part = base_part(4 + j)
        for i in range(2):
            total = part[256 * i:256 * (i + 1)] + mate_recv[j, i].astype(F32)
            if j < 3:
                q[j, i] = total.astype(BF)
            else:
                base_own[i] = total

    def x_copy(n, src, dst, way):
        return remote(src, dst, x_send_sem.at[n], x_recv_sem.at[n], x_dev[way])

    x_first = [x_copy(w, q.at[0, w], x_half.at[w], w) for w in range(2)]
    x_plain = [x_copy(2 + w, q.at[1 + w, 1 - w], x_recv.at[w, 1 - w], w) for w in range(2)]
    x_added = [x_copy(4 + w, q.at[1 + w, w], x_recv.at[w, w], w) for w in range(2)]

    base_mine(0)
    for copy in x_first:
        go(copy)
    base_mine(1)
    go(x_plain[0])
    base_mine(2)
    go(x_plain[1])
    z_serve(STREAM_A, 0)
    base_mine(3)

    for copy in s_copies:
        copy.wait_recv()
    for slot in range(4):
        for block in range(4):
            row = s_all[slot, 0:1, 128 * block:128 * (block + 1)]
            tile = jnp.broadcast_to(row, (128, 128)).T
            s_bc[slot, 128 * block:128 * (block + 1)] = tile

    z_serve(STREAM_A, 1)
    for way in range(2):
        y_tok[way][0].wait_recv()
        go(y_tok[way][2])
    for way in range(2):
        x_first[way].wait_recv()
        q[1 + way, way] = (q[1 + way, way].astype(F32) + x_half[way].astype(F32)).astype(BF)
        go(x_added[way])

    quarter = lax.broadcasted_iota(jnp.int32, (512, 128), 1) // 64

    def first_row(slot):
        d = 4 if slot == 7 else (-slot if slot < 4 else slot - 3)
        return at_z(d) * 16 + y * 4

    def low(slot, lowest, highest):
        rows = [(first_row(slot) + 2 * h + quarter).astype(F32) for h in range(2)]

        @pl.loop(lowest, highest)
        def _(i):
            product = lax.dot_general(tok_all[i], a_all[slot], NT, preferred_element_type=F32)
            for h in range(2):
                kept = jnp.where(s_bc[i] == rows[h], product[:, 128 * h:128 * (h + 1)], 0.0)
                if slot == 0:
                    acc[i, :, 128 * h:128 * (h + 1)] = kept
                else:
                    acc[i, :, 128 * h:128 * (h + 1)] += kept

    a_local.wait()
    for slot in (0, 1, 4):
        low(slot, 0, 1)
    z_serve(STREAM_A, 2)
    z_serve(STREAM_A, 3)
    for way in range(2):
        y_tok[way][1].wait_recv()
    for slot in (0, 1, 4):
        low(slot, 1, 3)
    for slot in (2, 5):
        low(slot, 0, 3)
    z_serve(STREAM_A, 4)
    for way in range(2):
        y_tok[way][2].wait_recv()
    for slot in (0, 1, 4, 2, 5):
        low(slot, 3, 4)
    z_serve(STREAM_A, 5)
    low(3, 0, 4)
    z_begin(1, 0, 1)
    low(6, 0, 4)
    z_serve(STREAM_A, 6)
    z_begin(2, 0)

    lane = lax.broadcasted_iota(jnp.int32, (256, 128), 1)

    def folded(i, half):
        rows = slice(256 * half, 256 * (half + 1))
        h = acc[i, rows, 0:128] + acc[i, rows, 128:256]
        return h + pltpu.roll(h, 64, 1)

    def pack(one, other):
        return jnp.where(lane < 64, folded(*one), folded(*other))

    def partial_copies(group):
        return [
            remote(
                packed[group].at[lax.rem(t + k, 8)], part_recv[group].at[k - 1],
                p_send.at[7 * group + k - 1], p_recv.at[7 * group + k - 1], others[k - 1],
            )
            for k in range(1, 8)
        ]

    p_copies = [partial_copies(group) for group in range(2)]

    def add_up(group):
        for copy in p_copies[group]:
            copy.wait_recv()
        total = packed[group][t]
        for k in range(7):
            total += part_recv[group][k]
        low_all[group][t] = total.astype(BF)
        for k in range(1, 8):
            go(remote(
                low_all[group].at[t], low_all[group].at[t],
                g_send.at[7 * group + k - 1], g_recv.at[7 * group + k - 1], others[k - 1],
            ))

    def collect(group):
        for k in range(1, 8):
            remote(
                low_all[group].at[t], low_all[group].at[lax.rem(t + 8 - k, 8)],
                g_send.at[7 * group + k - 1], g_recv.at[7 * group + k - 1], others[k - 1],
            ).wait_recv()

    low(7, 3, 4)
    packed[0][...] = pack((3, 0), (3, 1)).reshape(8, 32, 128)
    for copy in p_copies[0]:
        go(copy)
    z_serve(1, 0)
    low(7, 0, 3)
    z_serve(1, 1)
    z_begin(2, 1)
    pieces = [pack((1, 0), (2, 0)), pack((1, 1), (2, 1)), pack((0, 0), (0, 1))]
    packed[1][...] = jnp.concatenate(pieces, axis=0).reshape(8, 96, 128)
    for copy in p_copies[1]:
        go(copy)
    z_serve(1, 2)
    add_up(0)
    z_serve(1, 3)
    z_serve(2, 0)
    z_serve(1, 4)
    z_serve(2, 1)
    add_up(1)
    z_serve(1, 5)
    z_serve(1, 6)
    collect(0)

    def place(i):
        group, first = (0, 0) if i == 3 else (1, 512 if i == 0 else 0)
        v = low_all[group][...].astype(F32).reshape(-1, 128)[first:first + (512 if i in (1, 2) else 256)]
        turned = pltpu.roll(v, 64, 1)
        if i in (1, 2):
            left = lax.broadcasted_iota(jnp.int32, (512, 128), 1) < 64
            both = jnp.where(left, v, turned) if i == 1 else jnp.where(left, turned, v)
        else:
            both = jnp.concatenate([jnp.where(lane < 64, v, turned), jnp.where(lane < 64, turned, v)], axis=0)
        both = both.astype(BF)
        rows = s_bc[i].astype(BF)
        for slot in range(8):
            for h in range(2):
                want = (first_row(slot) + 2 * h + quarter).astype(BF)
                column = slot * 256 + 128 * h
                spread[i, :, column:column + 128] = jnp.where(rows == want, both, jnp.zeros_like(both))

    for copy in b_local:
        copy.wait()

    def r_copy(n, index, src, dst, way):
        i = n * 6 + index
        return remote(src, dst, r_send.at[i], r_recv.at[i], y_dev[way])

    r_first = [[r_copy(n, w, y_send[n].at[4 + w], y_half[n].at[w], w) for w in range(2)] for n in range(2)]
    r_plain = [
        [r_copy(n, 2 + w, y_send[n].at[2 * (1 - w) + 1 - w], y_recv[n].at[w, 1 - w], w) for w in range(2)]
        for n in range(2)
    ]
    r_added = [
        [r_copy(n, 4 + w, y_send[n].at[2 * (1 - w) + w], y_recv[n].at[w, w], w) for w in range(2)]
        for n in range(2)
    ]

    def adapted(n, i):
        return jnp.dot(spread[i], b_all[n][...], preferred_element_type=F32)

    def to_send(n, i):
        part = adapted(n, i).astype(BF)
        y_send[n][2 * i - 2] = part[0:256]
        y_send[n][2 * i - 1] = part[256:512]

    def send_first(n):
        for way in range(2):
            part = jnp.dot(spread[3, 256 * way:256 * (way + 1)], b_all[n][...], preferred_element_type=F32)
            y_send[n][4 + way] = part.astype(BF)
            go(r_first[n][way])

    def send_plain(n, way):
        to_send(n, 2 - way)
        go(r_plain[n][way])

    def send_added(n):
        for way in range(2):
            r_first[n][way].wait_recv()
            at = 2 * (1 - way) + way
            y_send[n][at] = (y_send[n][at].astype(F32) + y_half[n][way].astype(F32)).astype(BF)
            go(r_added[n][way])

    def mine(n):
        part = adapted(n, 0)
        own_adapted[n][0] = part[0:256]
        own_adapted[n][1] = part[256:512]

    def finish(n):
        for way in range(2):
            r_plain[n][way].wait_recv()
            r_added[n][way].wait_recv()
        first, width = CUTS[n]
        for i in range(2):
            extra = own_adapted[n][i] + (y_recv[n][0, i].astype(F32) + y_recv[n][1, i].astype(F32))
            out_ref[256 * i:256 * (i + 1), first:first + width] = (
                base_own[i, :, first:first + width] + 2.0 * extra
            ).astype(BF)

    place(3)
    send_first(0)
    z_serve(2, 2)
    collect(1)
    place(2)
    send_plain(0, 0)
    z_serve(2, 3)
    place(1)
    send_plain(0, 1)
    z_serve(2, 4)
    send_added(0)
    place(0)
    mine(0)
    for way in range(2):
        x_plain[way].wait_recv()
        x_added[way].wait_recv()
    for i in range(2):
        base_own[i] += x_recv[0, i].astype(F32) + x_recv[1, i].astype(F32)
    z_serve(2, 5)
    z_serve(2, 6)
    send_first(1)
    send_plain(1, 0)
    send_plain(1, 1)
    send_added(1)
    mine(1)
    finish(0)
    finish(1)
    for copy in started:
        copy.wait_send()


def body(
    tokens,
    projection_weight,
    adapter_input_maps,
    adapter_output_maps,
    adapter_store_row,
    adapter_lists_by_batch,
    request_list_position,
):
    dma = pltpu.SemaphoreType.DMA
    vmem = pltpu.VMEM
    hbm = pl.BlockSpec(memory_space=pl.ANY)
    near = pl.BlockSpec(memory_space=pltpu.VMEM)
    return pl.pallas_call(
        kernel,
        out_shape=jax.ShapeDtypeStruct((512, 512), BF),
        in_specs=[hbm] * 4 + [near] * 3,
        out_specs=near,
        scratch_shapes=[
            vmem((4, 512, 1024), BF),
            vmem((8, 256, 1024), BF),
            *[vmem((2048, width), BF) for _, width in CUTS],
            vmem((4, 8, 512), F32),
            vmem((4, 512, 128), F32),
            vmem((8, 1024, 512), BF),
            vmem((4, 512, 256), F32),
            vmem((4, 2, 256, 512), BF),
            vmem((4, 2, 256, 512), BF),
            vmem((3, 2, 256, 512), BF),
            vmem((2, 256, 512), F32),
            vmem((2, 256, 512), BF),
            vmem((2, 2, 256, 512), BF),
            vmem((8, 32, 128), F32),
            vmem((8, 96, 128), F32),
            vmem((7, 32, 128), F32),
            vmem((7, 96, 128), F32),
            vmem((8, 32, 128), BF),
            vmem((8, 96, 128), BF),
            vmem((4, 512, 2048), BF),
            *[
                scratch
                for _, width in CUTS
                for scratch in (
                    vmem((6, 256, width), BF),
                    vmem((2, 256, width), BF),
                    vmem((2, 2, 256, width), BF),
                    vmem((2, 256, width), F32),
                )
            ],
            dma((5,)), dma((8,)), dma((42,)), dma((42,)), dma((6,)), dma((6,)), dma((3,)), dma((3,)),
            dma((4,)), dma((4,)), dma((6,)), dma((6,)), dma((14,)), dma((14,)), dma((14,)), dma((14,)),
            dma((12,)), dma((12,)),
        ],
        compiler_params=pltpu.CompilerParams(
            collective_id=0, has_side_effects=True, vmem_limit_bytes=56 * 1024 * 1024
        ),
        cost_estimate=pl.CostEstimate(flops=17_200_000_000, bytes_accessed=13_000_000, transcendentals=0),
    )(
        tokens,
        projection_weight,
        jnp.swapaxes(adapter_input_maps, 1, 2).reshape(256, 1024),
        adapter_output_maps.reshape(256, 512),
        adapter_store_row.reshape(1, 128),
        adapter_lists_by_batch,
        request_list_position.reshape(1, 512),
    )


def solution(mesh):
    in_specs = (
        P("batch", "tensor"),
        P("tensor", None),
        P("batch", "tensor", None),
        P("batch", None, "tensor"),
        P(),
        P("batch", None),
        P("batch", None),
    )
    out_specs = P("batch", "tensor")
    return jax.shard_map(body, mesh=mesh, in_specs=in_specs, out_specs=out_specs, check_vma=False)
```

time: 99.1 us -> 91.3 us (0.921); the launches traced: 98.9 us -> 89.9 us
  Pallas kernels: 97.1 us -> 88 us
    pallas_call x1, Pallas kernels: 97.1 us -> 88 us  [body(): pl.pallas_call(kernel, out_shape=jax.ShapeDtypeStruct((512, 512), BF), in...]
where the time goes in v2:
time: 91.3 us; the launch traced here: 89.9 us
  Pallas kernels  88 us (96%)
  local copies, waits for them, and re-layouts  1.87 us (2%)
    pallas_call x1, Pallas kernels, body(): pl.pallas_call(kernel, out_shape=jax.ShapeDtypeStruct((512, 512), BF), in...  88 us
    unnamed x1, local copies, waits for them, and re-layouts  1.87 us

profile of v2, /device:TPU:1, one launch (start us, length us, event | category | flops | bytes accessed | tf_op | source)
XLA Modules:
  0.0 89.9 jit_solution(11060742367264946533)
XLA Ops:
  0.0 88.0 %shard_map.73 = bf16[512,512]{1,0:T(8,128)(2,1)} custom-call(bf16[512,1024]{1,0:T(8,128)(2,1)} %tok_h.1, bf16[1024,4096]{1,0:T(8,128)(2,1)} %w_h.1, bf16[256,1024]{1,0:T(8,128)(2,1)} %bitcast.6, bf16[256,512]{1,0:T(8,128)(2,1)} %bitcast.7, s32[1,128]{1,0:T(1,128)} %bitcast.9, s32[1,32]{1,0:T(1,128)} %list_ref.1, s32[1,512]{1,0:T(1,128)} %bitcast.8), custom_call_target="tpu_custom_call" | custom-call | flops 17200001024 | bytes 13000000 | tf_op jit(solution)/shard_map/pallas_call | solution.py:446
  88.0 1.9 %copy.9 = bf16[512,512]{1,0:T(8,128)(2,1)} copy(bf16[512,512]{1,0:T(8,128)(2,1)} %shard_map.73) | data formatting | bytes 1048576

commit v3 on v2

--- a/solution.py
+++ b/solution.py
@@ -146,9 +146,9 @@
 
     y_tok = [[y_copy(w, k) for k in range(3)] for w in range(2)]
 
+    z_begin(STREAM_A, 0, 1)
     for copy in s_copies:
         go(copy)
-    z_begin(STREAM_A, 0, 1)
     for k in range(2):
         for way in range(2):
             go(y_tok[way][k])
@@ -253,12 +253,12 @@
         y_tok[way][2].wait_recv()
     for slot in (0, 1, 4, 2, 5):
         low(slot, 3, 4)
+    z_begin(1, 0, 1)
     z_serve(STREAM_A, 5)
     low(3, 0, 4)
-    z_begin(1, 0, 1)
+    z_begin(2, 0)
     low(6, 0, 4)
     z_serve(STREAM_A, 6)
-    z_begin(2, 0)
 
     lane = lax.broadcasted_iota(jnp.int32, (256, 128), 1)
 
@@ -321,6 +321,7 @@
     z_serve(2, 1)
     add_up(1)
     z_serve(1, 5)
+    z_serve(2, 2)
     z_serve(1, 6)
     collect(0)
 
@@ -401,14 +402,13 @@
 
     place(3)
     send_first(0)
-    z_serve(2, 2)
+    z_serve(2, 3)
     collect(1)
     place(2)
     send_plain(0, 0)
-    z_serve(2, 3)
+    z_serve(2, 4)
     place(1)
     send_plain(0, 1)
-    z_serve(2, 4)
     send_added(0)
     place(0)
     mine(0)

time: 91.3 us -> 90.2 us (0.988); the launches traced: 89.9 us -> 90.1 us
  no operation moved by 1% of the time
where the time goes in v3:
time: 90.2 us; the launch traced here: 90.1 us
  Pallas kernels  88.2 us (98%)
  local copies, waits for them, and re-layouts  1.87 us (2%)
    pallas_call x1, Pallas kernels, body(): pl.pallas_call(kernel, out_shape=jax.ShapeDtypeStruct((512, 512), BF), in...  88.2 us
    unnamed x1, local copies, waits for them, and re-layouts  1.87 us

profile of v3, /device:TPU:1, one launch (start us, length us, event | category | flops | bytes accessed | tf_op | source)
XLA Modules:
  0.0 90.1 jit_solution(1895548836705813219)
XLA Ops:
  0.0 88.2 %shard_map.73 = bf16[512,512]{1,0:T(8,128)(2,1)} custom-call(bf16[512,1024]{1,0:T(8,128)(2,1)} %tok_h.1, bf16[1024,4096]{1,0:T(8,128)(2,1)} %w_h.1, bf16[256,1024]{1,0:T(8,128)(2,1)} %bitcast.6, bf16[256,512]{1,0:T(8,128)(2,1)} %bitcast.7, s32[1,128]{1,0:T(1,128)} %bitcast.9, s32[1,32]{1,0:T(1,128)} %list_ref.1, s32[1,512]{1,0:T(1,128)} %bitcast.8), custom_call_target="tpu_custom_call" | custom-call | flops 17200001024 | bytes 13000000 | tf_op jit(solution)/shard_map/pallas_call | solution.py:446
  88.2 1.9 %copy.9 = bf16[512,512]{1,0:T(8,128)(2,1)} copy(bf16[512,512]{1,0:T(8,128)(2,1)} %shard_map.73) | data formatting | bytes 1048576

commit v4 on v3

--- a/solution.py
+++ b/solution.py
@@ -249,11 +249,11 @@
     for slot in (2, 5):
         low(slot, 0, 3)
     z_serve(STREAM_A, 4)
+    z_begin(1, 0, 1)
     for way in range(2):
         y_tok[way][2].wait_recv()
     for slot in (0, 1, 4, 2, 5):
         low(slot, 3, 4)
-    z_begin(1, 0, 1)
     z_serve(STREAM_A, 5)
     low(3, 0, 4)
     z_begin(2, 0)

time: 90.2 us -> 90.2 us (level)
  no operation moved by 1% of the time
where the time goes in v4:
time: 90.2 us; the launch traced here: 90.1 us
  Pallas kernels  88.2 us (98%)
  local copies, waits for them, and re-layouts  1.87 us (2%)
    pallas_call x1, Pallas kernels, body(): pl.pallas_call(kernel, out_shape=jax.ShapeDtypeStruct((512, 512), BF), in...  88.2 us
    unnamed x1, local copies, waits for them, and re-layouts  1.87 us

profile of v4, /device:TPU:1, one launch (start us, length us, event | category | flops | bytes accessed | tf_op | source)
XLA Modules:
  0.0 90.1 jit_solution(5905568082197898654)
XLA Ops:
  0.0 88.2 %shard_map.73 = bf16[512,512]{1,0:T(8,128)(2,1)} custom-call(bf16[512,1024]{1,0:T(8,128)(2,1)} %tok_h.1, bf16[1024,4096]{1,0:T(8,128)(2,1)} %w_h.1, bf16[256,1024]{1,0:T(8,128)(2,1)} %bitcast.6, bf16[256,512]{1,0:T(8,128)(2,1)} %bitcast.7, s32[1,128]{1,0:T(1,128)} %bitcast.9, s32[1,32]{1,0:T(1,128)} %list_ref.1, s32[1,512]{1,0:T(1,128)} %bitcast.8), custom_call_target="tpu_custom_call" | custom-call | flops 17200001024 | bytes 13000000 | tf_op jit(solution)/shard_map/pallas_call | solution.py:446
  88.2 1.9 %copy.9 = bf16[512,512]{1,0:T(8,128)(2,1)} copy(bf16[512,512]{1,0:T(8,128)(2,1)} %shard_map.73) | data formatting | bytes 1048576
